TPU v7x, 32 devices: a whole 2x2x4 slice. The times are simulated.
32 devices in a mesh: grp: 2 (over y), dp: 16 (over z, x, core).
Axes of the slice: x: 2, y: 2, z: 4, core: 2. Of those that a mesh axis runs over, the one named last changes fastest.
Arguments:
- acts: bfloat16 [16384, 2560], P(('grp', 'dp')), may hold values from -18 to 18
- cotangents: bfloat16 [16384, 768], P(('grp', 'dp')), may hold values from -6 to 6
Outputs:
- update: float32 [2560, 768], P(('grp', 'dp'))
All inputs are finite; a program needn't handle non-finite values. Where the computation divides by a largest or mean magnitude, that divisor is 1e-20 or more.
Results may differ from a plain program's by a relative error of at most 0.013.
Values may be sent and summed in bfloat16 or wider, within the bound.
A program may use at most 64 MiB of HBM per device.

v0:
```python
import jax
import jax.numpy as jnp
from jax import lax
from jax.sharding import PartitionSpec as P

D = 2560
R = 768
BLK = 128
ITERS = 8


def newton_inverse(blocks):
    eye = jnp.eye(BLK, dtype=jnp.float32)
    trace = jnp.sum(blocks * eye, axis=(1, 2))
    damped = blocks + (0.1 * (trace / BLK + 1e-06))[:, None, None] * eye
    scale = 1.0 / jnp.max(jnp.sum(jnp.abs(damped), axis=2), axis=1)
    approx = scale[:, None, None] * eye
    for step in range(ITERS):
        product = jnp.einsum("nij,njk->nik", damped, approx, precision=lax.Precision.HIGHEST)
        approx = jnp.einsum(
            "nij,njk->nik", approx, 2.0 * eye - product, precision=lax.Precision.HIGHEST
        )
    return approx


def per_device(acts, cotangents):
    tokens = acts.shape[0]
    groups = lax.axis_size("grp")
    width_dp = lax.axis_size("dp")
    total = tokens * groups * width_dp
    in_blocks = D // BLK
    out_blocks = R // BLK
    all_blocks = in_blocks + out_blocks
    slots = (all_blocks + groups - 1) // groups
    padded_count = slots * groups
    x_blocks = acts.reshape(tokens, in_blocks, BLK)
    d_blocks = cotangents.reshape(tokens, out_blocks, BLK)
    fa = jnp.einsum("tbi,tbj->bij", x_blocks, x_blocks, preferred_element_type=jnp.float32) / total
    fg = jnp.einsum("tbi,tbj->bij", d_blocks, d_blocks, preferred_element_type=jnp.float32) / total
    filler = jnp.zeros((padded_count - all_blocks, BLK, BLK), jnp.float32)
    stacked = jnp.concatenate([fa, fg, filler], axis=0)
    owned = lax.psum_scatter(stacked, "grp", scatter_dimension=0, tiled=True)
    owned = lax.psum(owned, "dp")
    owned_inverse = newton_inverse(owned).astype(jnp.bfloat16)
    inverse16 = lax.all_gather(owned_inverse, "grp", axis=0, tiled=True)[:all_blocks]
    xpre = jnp.einsum(
        "tbi,bij->tbj", x_blocks, inverse16[:in_blocks], preferred_element_type=jnp.float32
    )
    xpre = xpre.astype(jnp.bfloat16).reshape(tokens, D)
    row_count = D // (groups * width_dp)
    mine = lax.psum_scatter(
        jnp.dot(xpre.T, cotangents, preferred_element_type=jnp.float32) / total,
        ("grp", "dp"),
        scatter_dimension=0,
        tiled=True,
    )
    out_inverse = inverse16[in_blocks:].astype(jnp.float32)
    natural = jnp.einsum(
        "rci,cij->rcj",
        mine.reshape(row_count, out_blocks, BLK),
        out_inverse,
        precision=lax.Precision.HIGHEST,
    ).reshape(row_count, R)
    quad = lax.psum(jnp.sum(natural * natural), ("grp", "dp")) / (D * R)
    return natural / jnp.sqrt(quad + 1e-06)


def solution(mesh):
    in_specs = (P(("grp", "dp"), None), P(("grp", "dp"), None))
    out_specs = P(("grp", "dp"), None)
    return jax.shard_map(
        per_device, mesh=mesh, in_specs=in_specs, out_specs=out_specs, check_vma=False
    )
```

profile of v0, /device:TPU:0, one launch (start us, length us, event | category | flops | bytes accessed | tf_op | source)
XLA Modules:
  0.0 350.6 jit_solution(1158352562578735457)
XLA Ops:
  6.5 0.0 reduce-scatter.3.cloned.1.call-start
  6.5 1.4 copy.28
  7.9 0.4 convolution_multiply_fusion.2
  8.3 3.0 copy.26
  11.3 0.8 convolution_multiply_fusion.1
  12.2 1.3 pad_maximum_fusion
  13.5 0.0 reduce-scatter.3.cloned.1.call-update
  13.5 0.0 all-reduce.2.cloned.1.call-start
  13.6 30.3 %reduce-scatter.3.cloned.1.call-done = f32[13,128,128]{2,1,0:T(8,128)} async-done(((f32[26,128,128]{2,1,0:T(8,128)}), f32[13,128,128]{2,1,0:T(8,128)}) %reduce-scatter.3.cloned.1.call-update) | async-done | bytes 851984 | tf_op jit(solution)/shard_map/reduce_scatter | solution.py:42
  43.9 0.0 all-reduce.2.cloned.1.call-update
  43.9 0.0 reduce-scatter.5.cloned.1.call-start
  44.0 0.6 fusion.10
  44.6 95.2 %all-reduce.2.cloned.1.call-done = f32[13,128,128]{2,1,0:T(8,128)} async-done(((f32[13,128,128]{2,1,0:T(8,128)}), f32[13,128,128]{2,1,0:T(8,128)}) %all-reduce.2.cloned.1.call-update) | async-done | bytes 851984 | tf_op jit(solution)/shard_map/psum | solution.py:43
  139.8 0.0 copy-start
  139.8 1.4 multiply_reduce_fusion
  141.2 1.5 abs_reduce_fusion
  142.8 0.1 reduce_max.9
  142.9 0.0 copy-start.1
  142.9 2.3 convolution_subtract_fusion.7
  145.2 1.0 fusion
  146.2 0.0 copy-done
  146.2 0.0 copy-done.1
  146.2 1.0 convolution_subtract_fusion.6
  147.3 0.9 fusion.12
  148.3 1.0 convolution_subtract_fusion.5
  149.3 0.9 fusion.13
  150.3 1.0 convolution_subtract_fusion.4
  151.3 0.9 fusion.14
  152.3 1.0 convolution_subtract_fusion.3
  153.3 0.9 fusion.15
  154.3 1.0 convolution_subtract_fusion.2
  155.3 1.1 fusion.16
  156.5 1.0 convolution_subtract_fusion.1
  157.5 0.9 fusion.17
  158.5 1.0 convolution_subtract_fusion
  159.5 0.9 convolution_convert_fusion.1
  160.5 12.2 %all_gather.3 = bf16[26,128,128]{2,1,0:T(8,128)(2,1)S(1)} all-gather(bf16[13,128,128]{2,1,0:T(8,128)(2,1)S(1)} %convolution_convert_fusion.1), channel_id=1, replica_groups=mesh['grp'=2,'dp'=16] {'grp'}, dimensions={0}, use_global_device_ids=true | all-gather | bytes 1277952 | tf_op jit(solution)/shard_map/all_gather | solution.py:45
  172.6 0.0 copy-start.2
  172.6 0.9 convolution_convert_fusion
  173.5 0.2 copy-done.2
  173.8 5.3 %convolution_multiply_fusion = f32[2560,768]{1,0:T(8,128)} fusion(bf16[512,2560]{0,1:T(8,128)(2,1)S(1)} %bitcast.54, bf16[512,768]{1,0:T(8,128)(2,1)S(1)} %copy-done.2), kind=kOutput, calls=%fused_computation | convolution fusion | flops 2015232000 | bytes 11272192 | tf_op jit(solution)/shard_map/dot_general | solution.py:52
  179.1 0.0 reduce-scatter.5.cloned.1.call-update
  179.1 121.5 %reduce-scatter.5.cloned.1.call-done = f32[80,768]{1,0:T(8,128)} async-done(((f32[2560,768]{1,0:T(8,128)}), f32[80,768]{1,0:T(8,128)}) %reduce-scatter.5.cloned.1.call-update) | async-done | bytes 245776 | tf_op jit(solution)/shard_map/reduce_scatter | solution.py:51
  300.5 1.9 multiply_reduce_fusion.1
  302.4 40.3 %psum.15 = f32[]{:T(128)} all-reduce(f32[]{:T(128)} %get-tuple-element.5), channel_id=1, replica_groups=mesh['grp'=2,'dp'=16] {'grp','dp'}, use_global_device_ids=true, to_apply=%region_7.0 | all-reduce | flops 1 | bytes 8 | tf_op jit(solution)/shard_map/psum | solution.py:64
  343.4 0.7 copy_bitcast_fusion
  (3 shorter events, 0.0 us)
Async XLA Ops:
  6.5 37.3 %reduce-scatter.3.cloned.1.call-start = ((), (), s32[]{:S(2)}) async-start(), calls=%async_computation.2 | async-start | bytes 2555904 | tf_op jit(solution)/shard_map/reduce_scatter | solution.py:42
  13.5 126.3 %all-reduce.2.cloned.1.call-start = ((), (), s32[]{:S(2)}) async-start(), calls=%async_computation.3 | async-start | bytes 1703936 | tf_op jit(solution)/shard_map/psum | solution.py:43
  43.9 256.6 %reduce-scatter.5.cloned.1.call-start = ((), (), s32[]{:S(2)}) async-start(), calls=%async_computation.4 | async-start | bytes 8110080 | tf_op jit(solution)/shard_map/reduce_scatter | solution.py:51
  139.8 6.4 %copy-start = (f32[13,128,128]{2,1,0:T(8,128)S(1)}, f32[13,128,128]{2,1,0:T(8,128)}, u32[]{:S(2)}) copy-start(f32[13,128,128]{2,1,0:T(8,128)} %all-reduce.2.cloned.1.call-done) | copy-start | bytes 2555908
  142.9 3.3 copy-start.1
  172.6 1.1 copy-start.2
Sparse Core Ops, SparseCore 0:
  13.6 30.1 reduce-scatter.2
  47.7 92.0 all-reduce.1
  179.2 121.2 reduce-scatter.4
where the time goes:
time: 351 us
  waiting for transfers between devices  247 us (70%)
  blocking collectives  52.4 us (15%)
  matrix products  26.7 us (8%)
  between operations  14 us (4%)
  other arithmetic  5.79 us (2%)
  local copies, waits for them, and re-layouts  4.65 us (1%)
    reduce_scatter x1, waiting for transfers between devices, per_device(): lax.psum_scatter(jnp.dot(xpre.T, cotangents, preferred_element_type=jnp.f...  121 us
    psum x1, waiting for transfers between devices, per_device(): owned = lax.psum(owned, 'dp')  95.2 us
    psum x1, blocking collectives, per_device(): quad = lax.psum(jnp.sum(natural * natural), ('grp', 'dp')) / (D * R)  40.3 us
    reduce_scatter x1, waiting for transfers between devices, per_device(): owned = lax.psum_scatter(stacked, 'grp', scatter_dimension=0, tiled=True)  30.3 us
    all_gather x1, blocking collectives, per_device(): lax.all_gather(owned_inverse, 'grp', axis=0, tiled=True)[:all_blocks]  12.2 us
    dot_general x8, matrix products, newton_inverse(): jnp.einsum('nij,njk->nik', damped, approx, precision=lax.Precision.HIGHEST)  9.59 us
    dot_general x8, matrix products, newton_inverse(): jnp.einsum('nij,njk->nik', approx, 2.0 * eye - product, precision=lax.Pre...  7.83 us
  transfers between devices with their start and end apart: 3, of which 3 were waited for; matrix products, arithmetic and copies ran while one was open for 0% of the time, Pallas kernels for 0%

commit v1 on v0

--- a/solution.py
+++ b/solution.py
@@ -40,7 +40,7 @@
     filler = jnp.zeros((padded_count - all_blocks, BLK, BLK), jnp.float32)
     stacked = jnp.concatenate([fa, fg, filler], axis=0)
     owned = lax.psum_scatter(stacked, "grp", scatter_dimension=0, tiled=True)
-    owned = lax.psum(owned, "dp")
+    owned = jnp.sum(lax.all_gather(owned, "dp"), axis=0)
     owned_inverse = newton_inverse(owned).astype(jnp.bfloat16)
     inverse16 = lax.all_gather(owned_inverse, "grp", axis=0, tiled=True)[:all_blocks]
     xpre = jnp.einsum(

time: 351 us -> 370 us (1.054)
  waiting for transfers between devices: 247 us -> 260 us
  other arithmetic: 5.79 us -> 9.51 us
    all_gather x0 -> x1, waiting for transfers between devices: none -> 109 us  [per_device(): owned = jnp.sum(lax.all_gather(owned, 'dp'), axis=0)]
    psum x1 -> x0, waiting for transfers between devices: 95.2 us -> none  [per_device(): owned = lax.psum(owned, 'dp')]
    reduce_sum x0 -> x1, other arithmetic: none -> 6.12 us  [per_device(): owned = jnp.sum(lax.all_gather(owned, 'dp'), axis=0)]
where the time goes in v1:
time: 370 us
  waiting for transfers between devices  260 us (70%)
  blocking collectives  53 us (14%)
  matrix products  27.5 us (7%)
  between operations  14 us (4%)
  other arithmetic  9.51 us (3%)
  local copies, waits for them, and re-layouts  5.57 us (2%)
    reduce_scatter x1, waiting for transfers between devices, per_device(): lax.psum_scatter(jnp.dot(xpre.T, cotangents, preferred_element_type=jnp.f...  121 us
    all_gather x1, waiting for transfers between devices, per_device(): owned = jnp.sum(lax.all_gather(owned, 'dp'), axis=0)  109 us
    psum x1, blocking collectives, per_device(): quad = lax.psum(jnp.sum(natural * natural), ('grp', 'dp')) / (D * R)  40.4 us
    reduce_scatter x1, waiting for transfers between devices, per_device(): owned = lax.psum_scatter(stacked, 'grp', scatter_dimension=0, tiled=True)  30.3 us
    all_gather x1, blocking collectives, per_device(): lax.all_gather(owned_inverse, 'grp', axis=0, tiled=True)[:all_blocks]  12.7 us
    dot_general x8, matrix products, newton_inverse(): jnp.einsum('nij,njk->nik', damped, approx, precision=lax.Precision.HIGHEST)  9.31 us
    dot_general x8, matrix products, newton_inverse(): jnp.einsum('nij,njk->nik', approx, 2.0 * eye - product, precision=lax.Pre...  7.85 us
  transfers between devices with their start and end apart: 3, of which 3 were waited for; matrix products, arithmetic and copies ran while one was open for 0% of the time, Pallas kernels for 0%

profile of v1, /device:TPU:0, one launch (start us, length us, event | category | flops | bytes accessed | tf_op | source)
XLA Modules:
  0.0 370.0 jit_solution(18365474373020334810)
XLA Ops:
  6.5 0.0 reduce-scatter.3.cloned.1.call-start
  6.5 3.0 copy.26
  9.5 1.9 convolution_multiply_fusion.1
  11.4 1.4 copy.28
  12.9 0.0 copy-start.1
  12.9 0.4 convolution_multiply_fusion.2
  13.2 0.9 copy-done.1
  14.2 1.3 pad_maximum_fusion
  15.5 0.0 reduce-scatter.3.cloned.1.call-update
  15.5 0.0 all-gather.3.cloned.1.call-start
  15.5 30.3 %reduce-scatter.3.cloned.1.call-done = f32[13,128,128]{2,1,0:T(8,128)} async-done(((f32[26,128,128]{2,1,0:T(8,128)}), f32[13,128,128]{2,1,0:T(8,128)}) %reduce-scatter.3.cloned.1.call-update) | async-done | bytes 851984 | tf_op jit(solution)/shard_map/reduce_scatter | solution.py:42
  45.9 0.0 all-gather.3.cloned.1.call-update
  45.9 0.0 reduce-scatter.5.cloned.1.call-start
  46.0 0.6 fusion.10
  46.6 109.2 %all-gather.3.cloned.1.call-done = f32[208,128,128]{2,1,0:T(8,128)} async-done(((f32[13,128,128]{2,1,0:T(8,128)}), f32[208,128,128]{2,1,0:T(8,128)}) %all-gather.3.cloned.1.call-update) | async-done | bytes 13631504 | tf_op jit(solution)/shard_map/all_gather | solution.py:43
  155.8 6.1 %reduce_sum.36 = f32[13,128,128]{2,1,0:T(8,128)S(1)} reduce(f32[16,13,128,128]{3,2,1,0:T(8,128)} %bitcast.54, f32[]{:T(128)} %constant.11.clone.1), dimensions={0}, to_apply=%region_1.0 | reduce | flops 3194880 | bytes 14483460 | tf_op jit(solution)/shard_map/reduce_sum | solution.py:43
  161.9 0.2 multiply_reduce_fusion
  162.1 0.4 abs_reduce_fusion
  162.5 0.1 reduce_max.9
  162.6 0.0 copy-start
  162.7 2.0 convolution_subtract_fusion.7
  164.7 1.0 fusion
  165.7 0.0 copy-done
  165.7 1.0 convolution_subtract_fusion.6
  166.8 0.9 fusion.12
  167.7 1.0 convolution_subtract_fusion.5
  168.8 0.9 fusion.13
  169.7 1.0 convolution_subtract_fusion.4
  170.8 0.9 fusion.14
  171.7 1.0 convolution_subtract_fusion.3
  172.8 1.1 fusion.15
  173.9 1.0 convolution_subtract_fusion.2
  175.0 0.9 fusion.16
  175.9 1.0 convolution_subtract_fusion.1
  177.0 0.9 fusion.17
  178.0 1.0 convolution_subtract_fusion
  179.0 0.9 convolution_convert_fusion.1
  180.0 12.7 %all_gather.11 = bf16[26,128,128]{2,1,0:T(8,128)(2,1)S(1)} all-gather(bf16[13,128,128]{2,1,0:T(8,128)(2,1)S(1)} %convolution_convert_fusion.1), channel_id=1, replica_groups=mesh['grp'=2,'dp'=16] {'grp'}, dimensions={0}, use_global_device_ids=true | all-gather | bytes 1277952 | tf_op jit(solution)/shard_map/all_gather | solution.py:45
  192.6 0.0 copy-start.2
  192.6 0.9 convolution_convert_fusion
  193.5 0.2 copy-done.2
  193.8 5.3 %convolution_multiply_fusion = f32[2560,768]{1,0:T(8,128)} fusion(bf16[512,2560]{0,1:T(8,128)(2,1)S(1)} %bitcast.56, bf16[512,768]{1,0:T(8,128)(2,1)S(1)} %copy-done.2), kind=kOutput, calls=%fused_computation | convolution fusion | flops 2015232000 | bytes 11272192 | tf_op jit(solution)/shard_map/dot_general | solution.py:52
  199.0 0.0 reduce-scatter.5.cloned.1.call-update
  199.1 120.8 %reduce-scatter.5.cloned.1.call-done = f32[80,768]{1,0:T(8,128)} async-done(((f32[2560,768]{1,0:T(8,128)}), f32[80,768]{1,0:T(8,128)}) %reduce-scatter.5.cloned.1.call-update) | async-done | bytes 245776 | tf_op jit(solution)/shard_map/reduce_scatter | solution.py:51
  319.8 1.9 multiply_reduce_fusion.1
  321.7 40.4 %psum.7 = f32[]{:T(128)} all-reduce(f32[]{:T(128)} %get-tuple-element.5), channel_id=1, replica_groups=mesh['grp'=2,'dp'=16] {'grp','dp'}, use_global_device_ids=true, to_apply=%region_7.0 | all-reduce | flops 1 | bytes 8 | tf_op jit(solution)/shard_map/psum | solution.py:64
  362.7 0.7 copy_bitcast_fusion
  (3 shorter events, 0.0 us)
Async XLA Ops:
  6.5 39.3 %reduce-scatter.3.cloned.1.call-start = ((), (), s32[]{:S(2)}) async-start(), calls=%async_computation.2 | async-start | bytes 2555904 | tf_op jit(solution)/shard_map/reduce_scatter | solution.py:42
  12.9 1.3 copy-start.1
  15.5 140.3 %all-gather.3.cloned.1.call-start = ((), (), s32[]{:S(2)}) async-start(), calls=%async_computation.4 | async-start | bytes 14483456 | tf_op jit(solution)/shard_map/all_gather | solution.py:43
  45.9 273.9 %reduce-scatter.5.cloned.1.call-start = ((), (), s32[]{:S(2)}) async-start(), calls=%async_computation.3 | async-start | bytes 8110080 | tf_op jit(solution)/shard_map/reduce_scatter | solution.py:51
  162.6 3.0 copy-start
  192.6 1.1 copy-start.2
Sparse Core Ops, SparseCore 0:
  15.6 30.1 reduce-scatter.2
  48.4 107.3 all-gather.2
  199.2 120.5 reduce-scatter.4
